TPU v7x, 256 devices: a whole 4x4x8 slice. The times are simulated.
256 devices in a mesh: dp: 16 (over y, x_hi, core), mp: 16 (over x_lo, z).
Axes of the slice: x: 4 (x_hi: 2, x_lo: 2; x = x_hi * 2 + x_lo), y: 4, z: 8, core: 2. Of those that a mesh axis runs over, the one named last changes fastest.
Arguments:
- activations: bfloat16 [16384, 4096], P('dp', 'mp'), may hold values from -6 to 6
- out_grads: bfloat16 [16384, 512], P(('dp', 'mp')), may hold values from -6 to 6
- doc_slot: int32 [16384], P('dp'), may hold values from 0 to 7
- input_eigenvectors: bfloat16 [4096, 4096], P(None, 'mp'), as said below
- eigen_out: bfloat16 [512, 512], replicated, as said below
- query_tiles: bfloat16 [32, 512, 4096], P(None, 'dp', 'mp'), may hold values from -6 to 6
- query_pick: int32 [16], replicated, may hold values from 0 to 31, as said below
Outputs:
- preconditioned: bfloat16 [4096, 16, 512], P('mp', None, 'dp')
Inputs may be any that keep to these rules, and one draw needn't show every extreme that they name: `doc_slot`: numbers name documents within the row's own group. `query_pick`: 16 different indices, among them 0 and 31, in no particular order. `input_eigenvectors`: Real-valued basis matrix with columns of unequal length. `eigen_out`: Real-valued basis matrix with columns of unequal length.
All inputs are finite; a program needn't handle non-finite values.
Results may differ from a plain program's by a relative error of at most 0.011.
Values may be sent and summed in bfloat16 or wider, within the bound.
A program may use at most 64 MiB of HBM per device.

v0:
```python
import jax
import jax.numpy as jnp
from jax import lax
from jax.sharding import PartitionSpec as P

DOC_G = 8
DAMPING = 0.1


def shards(
    activations, out_grads, doc_slot, input_eigenvectors, eigen_out, query_tiles, query_pick
):
    local_cols = input_eigenvectors.shape[1]
    basis_part = input_eigenvectors
    rotated_in = jnp.dot(
        lax.all_gather(activations, "mp", axis=1, tiled=True),
        basis_part,
        preferred_element_type=jnp.float32,
    ).astype(jnp.bfloat16)
    rotated_out = jnp.dot(
        lax.all_gather(out_grads, "mp", axis=0, tiled=True),
        eigen_out,
        preferred_element_type=jnp.float32,
    ).astype(jnp.bfloat16)
    onehot = (doc_slot[None, :] == jnp.arange(DOC_G, dtype=jnp.int32)[:, None]).astype(jnp.bfloat16)
    masked_entries = onehot[:, :, None] * rotated_out[None]
    doc_grad = jnp.einsum(
        "nre,rk->nek", masked_entries, rotated_in, preferred_element_type=jnp.float32
    )
    partial_sq = jnp.sum(doc_grad * doc_grad, axis=0)
    owner_rows = query_tiles.shape[1]
    summed = lax.psum(partial_sq, "dp")
    owned = lax.dynamic_slice_in_dim(summed, lax.axis_index("dp") * owner_rows, owner_rows, 0)
    eigen_vals = owned / (DOC_G * lax.axis_size("dp"))
    chosen = jnp.take(query_tiles, query_pick, axis=0).astype(jnp.float32)
    rescaled_gradient = (chosen / (eigen_vals[None] + DAMPING)).astype(jnp.bfloat16)
    selected = rescaled_gradient.shape[0]
    flat_tiles = rescaled_gradient.reshape(selected * owner_rows, local_cols)
    basis_part = input_eigenvectors
    final_output = lax.psum_scatter(
        lax.dot_general(
            basis_part, flat_tiles, (((1,), (1,)), ((), ())), preferred_element_type=jnp.float32
        ),
        "mp",
        scatter_dimension=0,
        tiled=True,
    )
    return final_output.reshape(final_output.shape[0], selected, owner_rows).astype(jnp.bfloat16)


def solution(mesh):
    in_specs = (
        P("dp", "mp"),
        P(("dp", "mp"), None),
        P("dp"),
        P(None, "mp"),
        P(),
        P(None, "dp", "mp"),
        P(),
    )
    out_specs = P("mp", None, "dp")
    return jax.shard_map(shards, mesh=mesh, in_specs=in_specs, out_specs=out_specs, check_vma=False)
```

profile of v0, /device:TPU:1, one launch (start us, length us, event | category | flops | bytes accessed | tf_op | source)
XLA Modules:
  0.0 478.1 jit_solution(12855527956758220249)
XLA Ops:
  6.5 0.0 copy-start
  6.5 0.0 all-gather.3.cloned.1.call-start
  6.5 0.7 all-gather.3.cloned.1.call-update
  7.3 0.0 all-gather.5.cloned.1.call-start
  7.3 0.7 all-gather.5.cloned.1.call-update
  8.0 0.0 all-reduce.2.cloned.1.call-start
  8.1 0.7 fusion.8
  8.8 63.0 %all-gather.3.cloned.1.call-done = bf16[1024,512]{1,0:T(8,128)(2,1)} async-done(((bf16[64,512]{1,0:T(8,128)(2,1)}), bf16[1024,512]{1,0:T(8,128)(2,1)}) %all-gather.3.cloned.1.call-update) | async-done | bytes 1048592 | tf_op jit(solution)/shard_map/all_gather | solution.py:21
  71.8 3.2 convolution_convert_fusion
  75.0 125.3 %all-gather.5.cloned.1.call-done = bf16[1024,4096]{1,0:T(8,128)(2,1)} async-done(((bf16[1024,256]{1,0:T(8,128)(2,1)}), bf16[1024,4096]{1,0:T(8,128)(2,1)}) %all-gather.5.cloned.1.call-update) | async-done | bytes 8388624 | tf_op jit(solution)/shard_map/all_gather | solution.py:16
  200.3 0.0 copy-done
  200.3 13.3 %multiply_reduce_fusion = f32[512,256]{1,0:T(8,128)} fusion(bf16[1024,512]{0,1:T(8,128)(2,1)} %convolution_convert_fusion, bf16[8,1024]{1,0:T(8,128)(2,1)S(1)} %fusion.8, bf16[1024,4096]{1,0:T(8,128)(2,1)} %all-gather.5.cloned.1.call-done, bf16[4096,256]{1,0:T(8,128)(2,1)S(1)} %copy-done), kind=kOutput, calls=%fused_computation.4 | convolution fusion | flops 4301389824 | bytes 12075008 | tf_op jit(solution)/shard_map/nre,rk->nek/dot_general | solution.py:27
  213.6 0.0 all-reduce.2.cloned.1.call-update
  213.6 0.0 reduce-scatter.2.cloned.1.call-start
  213.7 0.1 broadcast_in_dim.21
  213.8 0.1 broadcast_in_dim.22
  213.9 0.6 gather_fusion
  214.4 147.4 %all-reduce.2.cloned.1.call-done = f32[512,256]{1,0:T(8,128)} async-done(((f32[512,256]{1,0:T(8,128)}), f32[512,256]{1,0:T(8,128)}) %all-reduce.2.cloned.1.call-update) | async-done | bytes 524304 | tf_op jit(solution)/shard_map/psum | solution.py:32
  361.8 0.8 multiply_add_fusion
  362.6 0.1 fusion.7
  362.7 4.5 convolution_bitcast_fusion
  367.2 0.0 reduce-scatter.2.cloned.1.call-update
  367.2 102.5 %reduce-scatter.2.cloned.1.call-done = f32[256,512]{0,1:T(8,128)} async-done(((f32[4096,512]{0,1:T(8,128)}), f32[256,512]{0,1:T(8,128)}) %reduce-scatter.2.cloned.1.call-update) | async-done | bytes 524304 | tf_op jit(solution)/shard_map/reduce_scatter | solution.py:40
  469.8 1.8 convert_element_type.32
  (7 shorter events, 0.0 us)
Async XLA Ops:
  6.5 193.7 %copy-start = (bf16[4096,256]{1,0:T(8,128)(2,1)S(1)}, bf16[4096,256]{1,0:T(8,128)(2,1)}, u32[]{:S(2)}) copy-start(bf16[4096,256]{1,0:T(8,128)(2,1)} %param.10) | copy-start | bytes 6291460
  6.5 65.3 %all-gather.3.cloned.1.call-start = ((), (), s32[]{:S(2)}) async-start(), calls=%async_computation.1 | async-start | bytes 1114112 | tf_op jit(solution)/shard_map/all_gather | solution.py:21
  7.3 193.0 %all-gather.5.cloned.1.call-start = ((), (), s32[]{:S(2)}) async-start(), calls=%async_computation.2 | async-start | bytes 8912896 | tf_op jit(solution)/shard_map/all_gather | solution.py:16
  8.0 353.8 %all-reduce.2.cloned.1.call-start = ((), (), s32[]{:S(2)}) async-start(), calls=%async_computation.3 | async-start | bytes 1048576 | tf_op jit(solution)/shard_map/psum | solution.py:32
  75.0 138.7 %copy-start.2 = (s32[16]{0:T(128)S(1)}, s32[16]{0:T(128)}, u32[]{:S(2)}) copy-start(s32[16]{0:T(128)} %param.13) | copy-start | bytes 196
  75.0 138.9 %copy-start.1 = (bf16[32,32,256]{2,1,0:T(8,128)(2,1)S(1)}, bf16[32,32,256]{2,1,0:T(8,128)(2,1)}, u32[]{:S(2)}) copy-start(bf16[32,32,256]{2,1,0:T(8,128)(2,1)} %param.12) | copy-start | bytes 1572868
  213.6 256.2 %reduce-scatter.2.cloned.1.call-start = ((), (), s32[]{:S(2)}) async-start(), calls=%async_computation.4 | async-start | bytes 8912896 | tf_op jit(solution)/shard_map/reduce_scatter | solution.py:40
Sparse Core Ops, SparseCore 0:
  9.1 62.6 all-gather.2
  73.5 126.7 all-gather.4
  213.7 148.0 all-reduce.1
  367.4 102.3 reduce-scatter.1
where the time goes:
time: 478 us
  waiting for transfers between devices  440 us (92%)
  matrix products  21 us (4%)
  between operations  13.2 us (3%)
    psum x1, waiting for transfers between devices, shards(): summed = lax.psum(partial_sq, 'dp')  147 us
    all_gather x1, waiting for transfers between devices, shards(): lax.all_gather(activations, 'mp', axis=1, tiled=True)  125 us
    reduce_scatter x1, waiting for transfers between devices, shards(): lax.psum_scatter(lax.dot_general(basis_part, flat_tiles, (((1,), (1,)), (...  103 us
    all_gather x1, waiting for transfers between devices, shards(): lax.all_gather(out_grads, 'mp', axis=0, tiled=True)  63 us
    dot_general x1, matrix products, shards(): jnp.einsum('nre,rk->nek', masked_entries, rotated_in, preferred_element_t...  13.3 us
  transfers between devices with their start and end apart: 4, of which 4 were waited for; matrix products, arithmetic and copies ran while one was open for 1% of the time, Pallas kernels for 0%

commit v1 on v0

--- a/solution.py
+++ b/solution.py
@@ -5,6 +5,11 @@
 
 DOC_G = 8
 DAMPING = 0.1
+
+
+def press_case(panel):
+    all_rows = lax.all_gather(panel, axis_name="dp")
+    return jnp.sum(all_rows, 0)
 
 
 def shards(
@@ -29,7 +34,7 @@
     )
     partial_sq = jnp.sum(doc_grad * doc_grad, axis=0)
     owner_rows = query_tiles.shape[1]
-    summed = lax.psum(partial_sq, "dp")
+    summed = press_case(partial_sq)
     owned = lax.dynamic_slice_in_dim(summed, lax.axis_index("dp") * owner_rows, owner_rows, 0)
     eigen_vals = owned / (DOC_G * lax.axis_size("dp"))
     chosen = jnp.take(query_tiles, query_pick, axis=0).astype(jnp.float32)

time: 478 us -> 413 us (0.86)
  waiting for transfers between devices: 440 us -> 371 us
    psum x1 -> x0, waiting for transfers between devices: 147 us -> none  [shards(): summed = lax.psum(partial_sq, 'dp')]
    all_gather x0 -> x1, waiting for transfers between devices: none -> 82.1 us  [press_case(): all_rows = lax.all_gather(panel, axis_name='dp')]
where the time goes in v1:
time: 413 us; the launch traced here: 412 us
  waiting for transfers between devices  371 us (90%)
  matrix products  21 us (5%)
  between operations  13.2 us (3%)
  other arithmetic  6.61 us (2%)
    all_gather x1, waiting for transfers between devices, shards(): lax.all_gather(activations, 'mp', axis=1, tiled=True)  125 us
    reduce_scatter x1, waiting for transfers between devices, shards(): lax.psum_scatter(lax.dot_general(basis_part, flat_tiles, (((1,), (1,)), (...  98.8 us
    all_gather x1, waiting for transfers between devices, press_case(): all_rows = lax.all_gather(panel, axis_name='dp')  82.1 us
    all_gather x1, waiting for transfers between devices, shards(): lax.all_gather(out_grads, 'mp', axis=0, tiled=True)  63.1 us
    dot_general x1, matrix products, shards(): jnp.einsum('nre,rk->nek', masked_entries, rotated_in, preferred_element_t...  13.3 us
  transfers between devices with their start and end apart: 4, of which 4 were waited for; matrix products, arithmetic and copies ran while one was open for 1% of the time, Pallas kernels for 0%

profile of v1, /device:TPU:1, one launch (start us, length us, event | category | flops | bytes accessed | tf_op | source)
XLA Modules:
  0.0 412.4 jit_solution(10779319688143455733)
XLA Ops:
  6.5 0.0 copy-start
  6.5 0.0 all-gather.5.cloned.1.call-start
  6.5 0.7 all-gather.5.cloned.1.call-update
  7.3 0.0 all-gather.7.cloned.1.call-start
  7.3 0.7 all-gather.7.cloned.1.call-update
  8.0 0.0 all-gather.9.cloned.1.call-start
  8.1 0.7 fusion.8
  8.7 63.1 %all-gather.5.cloned.1.call-done = bf16[1024,512]{1,0:T(8,128)(2,1)} async-done(((bf16[64,512]{1,0:T(8,128)(2,1)}), bf16[1024,512]{1,0:T(8,128)(2,1)}) %all-gather.5.cloned.1.call-update) | async-done | bytes 1048592 | tf_op jit(solution)/shard_map/all_gather | solution.py:26
  71.8 3.2 convolution_convert_fusion
  75.0 125.3 %all-gather.7.cloned.1.call-done = bf16[1024,4096]{1,0:T(8,128)(2,1)} async-done(((bf16[1024,256]{1,0:T(8,128)(2,1)}), bf16[1024,4096]{1,0:T(8,128)(2,1)}) %all-gather.7.cloned.1.call-update) | async-done | bytes 8388624 | tf_op jit(solution)/shard_map/all_gather | solution.py:21
  200.3 0.0 copy-done
  200.3 13.3 %multiply_reduce_fusion = f32[512,256]{1,0:T(8,128)} fusion(bf16[1024,512]{0,1:T(8,128)(2,1)} %convolution_convert_fusion, bf16[8,1024]{1,0:T(8,128)(2,1)S(1)} %fusion.8, bf16[1024,4096]{1,0:T(8,128)(2,1)} %all-gather.7.cloned.1.call-done, bf16[4096,256]{1,0:T(8,128)(2,1)S(1)} %copy-done), kind=kOutput, calls=%fused_computation.4 | convolution fusion | flops 4301389824 | bytes 12075008 | tf_op jit(solution)/shard_map/nre,rk->nek/dot_general | solution.py:32
  213.6 0.0 all-gather.9.cloned.1.call-update
  213.6 0.0 reduce-scatter.2.cloned.1.call-start
  213.7 0.1 broadcast_in_dim.21
  213.8 0.1 broadcast_in_dim.22
  213.9 0.6 gather_fusion
  214.4 82.1 %all-gather.9.cloned.1.call-done = f32[8192,256]{1,0:T(8,128)} async-done(((f32[512,256]{1,0:T(8,128)}), f32[8192,256]{1,0:T(8,128)}) %all-gather.9.cloned.1.call-update) | async-done | bytes 8388624 | tf_op jit(solution)/shard_map/all_gather | solution.py:11
  296.6 4.0 reduce_sum.19
  300.6 0.1 fusion.7
  300.7 4.5 %convolution_bitcast_fusion = f32[4096,512]{0,1:T(8,128)} fusion(bf16[512,256]{1,0:T(8,128)(2,1)S(1)} %fusion.7, bf16[4096,256]{1,0:T(8,128)(2,1)S(1)} %copy-done), kind=kOutput, calls=%fused_computation.3 | convolution fusion | flops 1073741824 | bytes 10747904 | tf_op jit(solution)/shard_map/dot_general | solution.py:46
  305.2 0.0 reduce-scatter.2.cloned.1.call-update
  305.3 98.8 %reduce-scatter.2.cloned.1.call-done = f32[256,512]{0,1:T(8,128)} async-done(((f32[4096,512]{0,1:T(8,128)}), f32[256,512]{0,1:T(8,128)}) %reduce-scatter.2.cloned.1.call-update) | async-done | bytes 524304 | tf_op jit(solution)/shard_map/reduce_scatter | solution.py:45
  404.1 1.8 convert_element_type.32
  (8 shorter events, 0.0 us)
Async XLA Ops:
  6.5 193.7 %copy-start = (bf16[4096,256]{1,0:T(8,128)(2,1)S(1)}, bf16[4096,256]{1,0:T(8,128)(2,1)}, u32[]{:S(2)}) copy-start(bf16[4096,256]{1,0:T(8,128)(2,1)} %param.10) | copy-start | bytes 6291460
  6.5 65.3 %all-gather.5.cloned.1.call-start = ((), (), s32[]{:S(2)}) async-start(), calls=%async_computation.1 | async-start | bytes 1114112 | tf_op jit(solution)/shard_map/all_gather | solution.py:26
  7.3 193.0 %all-gather.7.cloned.1.call-start = ((), (), s32[]{:S(2)}) async-start(), calls=%async_computation.2 | async-start | bytes 8912896 | tf_op jit(solution)/shard_map/all_gather | solution.py:21
  8.0 288.6 %all-gather.9.cloned.1.call-start = ((), (), s32[]{:S(2)}) async-start(), calls=%async_computation.4 | async-start | bytes 8912896 | tf_op jit(solution)/shard_map/all_gather | solution.py:11
  75.0 138.7 %copy-start.2 = (s32[16]{0:T(128)S(1)}, s32[16]{0:T(128)}, u32[]{:S(2)}) copy-start(s32[16]{0:T(128)} %param.13) | copy-start | bytes 196
  75.0 138.9 %copy-start.1 = (bf16[32,32,256]{2,1,0:T(8,128)(2,1)S(1)}, bf16[32,32,256]{2,1,0:T(8,128)(2,1)}, u32[]{:S(2)}) copy-start(bf16[32,32,256]{2,1,0:T(8,128)(2,1)} %param.12) | copy-start | bytes 1572868
  213.6 190.5 %reduce-scatter.2.cloned.1.call-start = ((), (), s32[]{:S(2)}) async-start(), calls=%async_computation.3 | async-start | bytes 8912896 | tf_op jit(solution)/shard_map/reduce_scatter | solution.py:45
Sparse Core Ops, SparseCore 0:
  9.1 62.6 all-gather.4
  73.5 126.7 all-gather.6
  213.7 82.7 all-gather.8
  305.4 98.6 reduce-scatter.1
